TPU v7x, 128 devices: a whole 4x4x4 slice. The times are simulated.
128 devices in a mesh: ctx: 32 (over y, z, core), tp: 4 (over x).
Axes of the slice: x: 4, y: 4, z: 4, core: 2. Of those that a mesh axis runs over, the one named last changes fastest.
Arguments:
- ctx_q: bfloat16 [24576, 8192], P('ctx', 'tp'), may hold values from -150 to 150
- ctx_k: bfloat16 [24576, 1024], P('ctx', 'tp'), may hold values from -8 to 8
- ctx_v: bfloat16 [24576, 1024], P('ctx', 'tp'), may hold values from -6 to 6
- query_q: bfloat16 [256, 8192], P('ctx', 'tp'), may hold values from -150 to 150
- query_k: bfloat16 [256, 1024], P('ctx', 'tp'), may hold values from -8 to 8
- query_v: bfloat16 [256, 1024], P('ctx', 'tp'), may hold values from -6 to 6
- out_weight: bfloat16 [8192, 8192], P('tp', 'ctx'), may hold values from -0.0625 to 0.0625
Outputs:
- ctx_out: bfloat16 [24576, 8192], P('ctx', 'tp')
- query_out: bfloat16 [256, 8192], P('tp', 'ctx')
All inputs are finite; a program needn't handle non-finite values.
Results may differ from a plain program's by a relative error of at most 0.011.
Values may be sent and summed in bfloat16 or wider, within the bound.
A program may use at most 320 MiB of HBM per device.

v0:
```python
import jax
import jax.numpy as jnp
from jax import lax
from jax.sharding import PartitionSpec as P

HEAD_DIM = 128


def from_root(value, axis, source):
    kept = jnp.where(lax.axis_index(axis) == source, value, 0).astype(value.dtype)
    return lax.psum(kept, axis)


def head_stats(queries, keys, values, mask):
    scores = jnp.einsum(
        "rgd,kd->rgk", queries, keys, preferred_element_type=jnp.float32
    ) * HEAD_DIM ** (-0.5)
    if mask is not None:
        scores = jnp.where(mask[:, None, :], scores, -1e30)
    top = jnp.max(scores, axis=2)
    weights = jnp.exp(scores - top[..., None])
    total = jnp.sum(weights, axis=2)
    mixed = jnp.einsum(
        "rgk,kd->rgd", weights.astype(jnp.bfloat16), values, preferred_element_type=jnp.float32
    )
    return (top, total, mixed)


def local_heads(queries, keys, values, mask):
    kv_local = keys.shape[1] // HEAD_DIM
    group = queries.shape[1] // keys.shape[1]
    rows = queries.shape[0]
    qh = queries.reshape(rows, kv_local, group, HEAD_DIM)
    kh = keys.reshape(keys.shape[0], kv_local, HEAD_DIM)
    vh = values.reshape(values.shape[0], kv_local, HEAD_DIM)
    tops, totals, mixes = ([], [], [])
    for head in range(kv_local):
        top, total, mixed = head_stats(qh[:, head], kh[:, head], vh[:, head], mask)
        tops.append(top)
        totals.append(total)
        mixes.append(mixed)
    return (jnp.concatenate(tops, 1), jnp.concatenate(totals, 1), jnp.concatenate(mixes, 1))


def encode_block(ctx_q, ctx_k, ctx_v, anchor_k, anchor_v, position):
    rows = ctx_q.shape[0]
    kv_local = ctx_k.shape[1] // HEAD_DIM
    group = ctx_q.shape[1] // ctx_k.shape[1]
    keys = jnp.concatenate([anchor_k, ctx_k], 0).reshape(2 * rows, kv_local, HEAD_DIM)
    values = jnp.concatenate([anchor_v, ctx_v], 0).reshape(2 * rows, kv_local, HEAD_DIM)
    qh = ctx_q.reshape(rows, kv_local, group, HEAD_DIM)
    row_ids = jnp.arange(rows, dtype=jnp.int32)[:, None]
    col_ids = jnp.arange(2 * rows, dtype=jnp.int32)[None, :]
    mask = jnp.where(col_ids < rows, position > 0, col_ids - rows <= row_ids)
    width = min(group, 4)
    pieces = []
    for head in range(kv_local):
        for first in range(0, group, width):
            top, total, mixed = head_stats(
                qh[:, head, first : first + width], keys[:, head], values[:, head], mask
            )
            pieces.append((mixed / total[..., None]).astype(jnp.bfloat16))
    return jnp.concatenate(pieces, 1).reshape(rows, ctx_q.shape[1])


def finish(top, total_sum, mixed_sum, queries, all_keys, all_values):
    count = queries.shape[0]
    row_ids = jnp.arange(count, dtype=jnp.int32)[:, None]
    col_ids = jnp.arange(all_keys.shape[0], dtype=jnp.int32)[None, :]
    self_top, self_total, self_mixed = local_heads(
        queries, all_keys, all_values, col_ids <= row_ids
    )
    peak = jnp.maximum(top, self_top)
    outer = jnp.exp(top - peak)
    inner = jnp.exp(self_top - peak)
    numer = outer[..., None] * mixed_sum + inner[..., None] * self_mixed
    denom = outer * total_sum + inner * self_total
    return (numer / denom[..., None]).astype(jnp.bfloat16).reshape(count, queries.shape[1])


def body(ctx_q, ctx_k, ctx_v, query_q, query_k, query_v, out_weight):
    anchor_k, anchor_v = (from_root(ctx_k, "ctx", 0), from_root(ctx_v, "ctx", 0))
    all_q, all_k, all_v = (
        lax.all_gather(query_q, "ctx", axis=0, tiled=True),
        lax.all_gather(query_k, "ctx", axis=0, tiled=True),
        lax.all_gather(query_v, "ctx", axis=0, tiled=True),
    )
    position = lax.axis_index("ctx")
    ctx_out = encode_block(ctx_q, ctx_k, ctx_v, anchor_k, anchor_v, position)
    top, total, mixed = local_heads(all_q, ctx_k, ctx_v, None)
    peak = lax.pmax(top, "ctx")
    factor = jnp.exp(top - peak)
    total_sum, mixed_sum = lax.psum((total * factor, mixed * factor[..., None]), "ctx")
    attn = finish(peak, total_sum, mixed_sum, all_q, all_k, all_v)
    query_out = lax.psum_scatter(
        jnp.dot(attn, out_weight, preferred_element_type=jnp.float32),
        "tp",
        scatter_dimension=0,
        tiled=True,
    ).astype(jnp.bfloat16)
    return (ctx_out, query_out)


def solution(mesh):
    return jax.shard_map(
        body,
        mesh=mesh,
        in_specs=(
            P("ctx", "tp"),
            P("ctx", "tp"),
            P("ctx", "tp"),
            P("ctx", "tp"),
            P("ctx", "tp"),
            P("ctx", "tp"),
            P("tp", "ctx"),
        ),
        out_specs=(P("ctx", "tp"), P("tp", "ctx")),
        check_vma=False,
    )
```

profile of v0, /device:TPU:1, one launch (start us, length us, event | category | flops | bytes accessed | tf_op | source)
XLA Modules:
  0.0 629.4 jit_solution(14238796037516414602)
XLA Ops:
  11.5 27.4 %all_gather.10 = bf16[256,256]{1,0:T(8,128)(2,1)S(1)} all-gather(bf16[8,256]{1,0:T(8,128)(2,1)} %param.11), channel_id=1, replica_groups=mesh['ctx'=32,'tp'=4] {'ctx'}, dimensions={0}, use_global_device_ids=true | all-gather | bytes 135168 | tf_op jit(solution)/shard_map/all_gather | solution.py:85
  39.0 24.0 %all_gather.11 = bf16[256,256]{1,0:T(8,128)(2,1)S(1)} all-gather(bf16[8,256]{1,0:T(8,128)(2,1)} %param.12), channel_id=1, replica_groups=mesh['ctx'=32,'tp'=4] {'ctx'}, dimensions={0}, use_global_device_ids=true | all-gather | bytes 135168 | tf_op jit(solution)/shard_map/all_gather | solution.py:86
  63.2 4.9 copy.57
  69.4 49.6 %all-reduce.6.cloned.1.call-done = (bf16[768,256]{0,1:T(8,128)(2,1)}, bf16[768,256]{0,1:T(8,128)(2,1)}) async-done(((bf16[768,256]{0,1:T(8,128)(2,1)}, bf16[768,256]{0,1:T(8,128)(2,1)}), (bf16[768,256]{0,1:T(8,128)(2,1)}, bf16[768,256]{0,1:T(8,128)(2,1)})) %all-reduce.6.cloned.1.call-update) | async-done | bytes 786448 | tf_op jit(solution)/shard_map/psum | solution.py:11
  120.1 9.2 %fusion.67 = f32[1536,768,4]{1,0,2:T(8,128)} fusion(bf16[768,2,8,128]{0,3,2,1:T(8,128)(2,1)} %bitcast.173, bf16[1536,2,128]{0,2,1:T(8,128)(2,1)S(1)} %bitcast.186), kind=kOutput, calls=%fused_computation.77 | convolution fusion | flops 1207959552 | bytes 20054016 | tf_op jit(solution)/shard_map/rgd,kd->rgk/dot_general | solution.py:15
  129.3 8.1 %fusion.66 = f32[1536,768,4]{1,0,2:T(8,128)} fusion(bf16[768,2,8,128]{0,3,2,1:T(8,128)(2,1)S(1)} %bitcast.175, bf16[1536,2,128]{0,2,1:T(8,128)(2,1)S(1)} %bitcast.187), kind=kOutput, calls=%fused_computation.75 | convolution fusion | flops 1207959552 | bytes 20054016 | tf_op jit(solution)/shard_map/rgd,kd->rgk/dot_general | solution.py:15
  138.3 8.3 %fusion.8 = (f32[768,4]{0,1:T(4,128)S(1)}, f32[1536,768,4]{1,0,2:T(8,128)}) fusion(pred[768,1536]{0,1:T(8,128)(4,1)S(1)} %fusion.28, bf16[768,2,8,128]{0,3,2,1:T(8,128)(2,1)S(1)} %bitcast.176, bf16[1536,2,128]{0,2,1:T(8,128)(2,1)S(1)} %bitcast.188), kind=kOutput, calls=%fused_computation.16 | convolution fusion | flops 1222112256 | bytes 21245952 | tf_op jit(solution)/shard_map/rgd,kd->rgk/dot_general | solution.py:15
  146.6 30.3 %fusion = (f32[768,4]{0,1:T(4,128)S(1)}, f32[768,4]{0,1:T(4,128)S(1)}, f32[768,4]{0,1:T(4,128)S(1)}, f32[768,4]{0,1:T(4,128)S(1)}, f32[1536,768,4]{1,0,2:T(8,128)}) fusion(f32[1536,768,4]{1,0,2:T(8,128)} %get-tuple-element.25, f32[768,4]{0,1:T(4,128)S(1)} %get-tuple-element.24, pred[768,1536]{0,1:T(8,128)(4,1)S(1)} %fusion.28, f32[1536,768,4]{1,0,2:T(8,128)} %fusion.67, ...), kind=kOutput, calls=%fused_computation.8 | convolution fusion | flops 1269288960 | bytes 77918208 | tf_op jit(solution)/shard_map/rgd,kd->rgk/dot_general | solution.py:15
  177.0 10.1 %divide_convert_fusion.3 = bf16[768,4,128]{0,2,1:T(8,128)(2,1)} fusion(f32[1536,768,4]{1,0,2:T(8,128)} %get-tuple-element.25, f32[768,4]{0,1:T(4,128)S(1)} %get-tuple-element.24, pred[768,1536]{0,1:T(8,128)(4,1)S(1)} %fusion.28, f32[768,4]{0,1:T(4,128)S(1)} %get-tuple-element.8, bf16[1536,2,128]{0,2,1:T(8,128)(2,1)} %bitcast.190), kind=kOutput, calls=%fused_computation.63 | convolution fusion | flops 1227620352 | bytes 21258240 | tf_op jit(solution)/shard_map/rgk,kd->rgd/dot_general | solution.py:23
  189.2 17.3 %fusion.2 = (f32[768,4]{0,1:T(4,128)S(1)}, f32[768,4]{0,1:T(4,128)S(1)}, f32[768,4]{0,1:T(4,128)S(1)}) fusion(f32[1536,768,4]{1,0,2:T(8,128)} %get-tuple-element.26, f32[768,4]{0,1:T(4,128)S(1)} %get-tuple-element.9, pred[768,1536]{0,1:T(8,128)(4,1)S(1)} %fusion.28, f32[768,4]{0,1:T(4,128)S(1)} %get-tuple-element.10, f32[1536,768,4]{1,0,2:T(8,128)S(1)} %bitcast.171, ...), kind=kLoop, calls=%fused_computation.10 | loop fusion | flops 56613888 | bytes 57876480 | tf_op jit(solution)/shard_map/reduce_sum | solution.py:22
  206.5 10.2 %divide_convert_fusion = bf16[768,4,128]{0,2,1:T(8,128)(2,1)} fusion(f32[1536,768,4]{1,0,2:T(8,128)} %fusion.66, f32[768,4]{0,1:T(4,128)S(1)} %get-tuple-element.11, pred[768,1536]{0,1:T(8,128)(4,1)S(1)} %fusion.28, f32[768,4]{0,1:T(4,128)S(1)} %get-tuple-element.14, bf16[1536,2,128]{0,2,1:T(8,128)(2,1)S(1)} %bitcast.191), kind=kOutput, calls=%fused_computation.60 | convolution fusion | flops 1227620352 | bytes 21258240 | tf_op jit(solution)/shard_map/rgk,kd->rgd/dot_general | solution.py:23
  216.8 6.0 divide_convert_fusion.1
  222.8 2.3 copy.69
  225.1 2.2 multiply_reduce_fusion.1
  228.4 2.3 fusion.31
  230.7 2.7 fusion.24
  233.5 2.3 fusion.29
  235.8 122.1 %pmax.7 = f32[256,16]{0,1:T(8,128)S(1)} all-reduce(f32[256,16]{0,1:T(8,128)S(1)} %pad_maximum_fusion.3), channel_id=1, replica_groups=mesh['ctx'=32,'tp'=4] {'ctx'}, use_global_device_ids=true, to_apply=%region_12.13 | all-reduce | flops 4096 | bytes 32768 | tf_op jit(solution)/shard_map/pmax | solution.py:91
  357.9 123.8 %psum.31 = f32[256,16]{0,1:T(8,128)S(1)} all-reduce(f32[256,16]{0,1:T(8,128)S(1)} %get-tuple-element.22), channel_id=1, replica_groups=mesh['ctx'=32,'tp'=4] {'ctx'}, use_global_device_ids=true, to_apply=%region_18.19 | all-reduce | flops 4096 | bytes 32768 | tf_op jit(solution)/shard_map/psum | solution.py:93
  481.7 2.9 maximum_multiply_fusion
  484.6 1.5 fusion.40
  486.2 1.9 fusion.42
  488.6 1.8 fusion.48
  490.4 1.8 fusion.46
  492.1 101.3 %all-reduce.4.cloned.1.call-done = f32[256,16,128]{2,0,1:T(8,128)} async-done(((f32[256,16,128]{2,0,1:T(8,128)}), f32[256,16,128]{2,0,1:T(8,128)}) %all-reduce.4.cloned.1.call-update) | async-done | bytes 2097168 | tf_op jit(solution)/shard_map/psum | solution.py:93
  593.4 4.9 fusion.39
  598.4 2.3 copy.86
  600.7 2.4 fusion.93
  603.2 9.5 %divide_convert_fusion.2 = bf16[768,4,128]{0,2,1:T(8,128)(2,1)S(1)} fusion(f32[1536,768,4]{1,0,2:T(8,128)} %get-tuple-element.26, f32[768,4]{0,1:T(4,128)S(1)} %get-tuple-element.9, pred[768,1536]{0,1:T(8,128)(4,1)S(1)} %fusion.28, f32[768,4]{0,1:T(4,128)S(1)} %get-tuple-element.12, bf16[1536,2,128]{0,2,1:T(8,128)(2,1)S(1)} %bitcast.193), kind=kOutput, calls=%fused_computation.62 | convolution fusion | flops 1227620352 | bytes 21258240 | tf_op jit(solution)/shard_map/rgk,kd->rgd/dot_general | solution.py:23
  612.6 1.9 pad_maximum_fusion
  614.5 4.6 copy.87
  619.1 2.0 reduce-scatter.2.cloned.1.call-done
  (57 shorter events, 12.9 us)
Async XLA Ops:
  7.2 593.5 %copy-start = (bf16[2048,256]{1,0:T(8,128)(2,1)S(1)}, bf16[2048,256]{1,0:T(8,128)(2,1)}, u32[]{:S(2)}) copy-start(bf16[2048,256]{1,0:T(8,128)(2,1)} %param.13) | copy-start | bytes 3145732
  7.2 111.8 %all-reduce.6.cloned.1.call-start = ((), (), s32[]{:S(2)}) async-start(), calls=%async_computation.4 | async-start | bytes 1572864 | tf_op jit(solution)/shard_map/psum | solution.py:11
  10.6 212.2 %all-gather.2.cloned.1.call-start = ((), (), s32[]{:S(2)}) async-start(), calls=%async_computation.1 | async-start | bytes 1081344 | tf_op jit(solution)/shard_map/all_gather | solution.py:84
  11.4 582.1 %all-reduce.4.cloned.1.call-start = ((), (), s32[]{:S(2)}) async-start(), calls=%async_computation.2 | async-start | bytes 4194304 | tf_op jit(solution)/shard_map/psum | solution.py:93
  120.0 18.3 %copy-start.3 = (bf16[1536,256]{0,1:T(8,128)(2,1)}, bf16[1536,256]{0,1:T(8,128)(2,1)S(1)}, u32[]{:S(2)}) copy-start(bf16[1536,256]{0,1:T(8,128)(2,1)S(1)} %pad_maximum_fusion.2) | copy-start | bytes 2359300
  120.1 9.2 %copy-start.1 = (bf16[768,2048]{0,1:T(8,128)(2,1)S(1)}, bf16[768,2048]{0,1:T(8,128)(2,1)}, u32[]{:S(2)}) copy-start(bf16[768,2048]{0,1:T(8,128)(2,1)} %copy.57) | copy-start | bytes 9437188
  129.3 8.1 %copy-start.9 = (bf16[768,256]{0,1:T(8,128)(2,1)S(1)}, bf16[768,256]{0,1:T(8,128)(2,1)}, u32[]{:S(2)}) copy-start(bf16[768,256]{0,1:T(8,128)(2,1)} %get-tuple-element.18) | copy-start | bytes 1179652
  177.0 10.1 %slice-start = ((s8[18874368]{0:T(1024)(128)(4,1)}), s8[4194304]{0:T(1024)(128)(4,1)S(1)}, s32[]{:S(2)}) async-start(s8[18874368]{0:T(1024)(128)(4,1)} %bitcast.170), calls=%async_computation.5 | async-start | bytes 8388608
  177.0 10.1 %slice-start.1 = ((s8[18874368]{0:T(1024)(128)(4,1)}), s8[4194304]{0:T(1024)(128)(4,1)S(1)}, s32[]{:S(2)}) async-start(s8[18874368]{0:T(1024)(128)(4,1)} %bitcast.170), calls=%async_computation.6 | async-start | bytes 8388608
  177.0 10.3 %slice-start.2 = ((s8[18874368]{0:T(1024)(128)(4,1)}), s8[4194304]{0:T(1024)(128)(4,1)S(1)}, s32[]{:S(2)}) async-start(s8[18874368]{0:T(1024)(128)(4,1)} %bitcast.170), calls=%async_computation.7 | async-start | bytes 8388608
  177.0 11.6 %slice-start.3 = ((s8[18874368]{0:T(1024)(128)(4,1)}), s8[4194304]{0:T(1024)(128)(4,1)S(1)}, s32[]{:S(2)}) async-start(s8[18874368]{0:T(1024)(128)(4,1)} %bitcast.170), calls=%async_computation.8 | async-start | bytes 8388608
  177.0 12.2 %slice-start.4 = ((s8[18874368]{0:T(1024)(128)(4,1)}), s8[2097152]{0:T(1024)(128)(4,1)S(1)}, s32[]{:S(2)}) async-start(s8[18874368]{0:T(1024)(128)(4,1)} %bitcast.170), calls=%async_computation.9 | async-start | bytes 4194304
  189.2 17.3 %copy-start.7 = (bf16[1536,256]{0,1:T(8,128)(2,1)S(1)}, bf16[1536,256]{0,1:T(8,128)(2,1)}, u32[]{:S(2)}) copy-start(bf16[1536,256]{0,1:T(8,128)(2,1)} %pad_maximum_fusion.1) | copy-start | bytes 2359300
  225.1 2.2 copy-start.2
  484.6 136.6 %reduce-scatter.2.cloned.1.call-start = ((), (), s32[]{:S(2)}) async-start(), calls=%async_computation.3 | async-start | bytes 327680 | tf_op jit(solution)/shard_map/reduce_scatter | solution.py:95
  593.4 9.7 %copy-start.8 = (bf16[1536,256]{0,1:T(8,128)(2,1)S(1)}, bf16[1536,256]{0,1:T(8,128)(2,1)}, u32[]{:S(2)}) copy-start(bf16[1536,256]{0,1:T(8,128)(2,1)} %pad_maximum_fusion.1) | copy-start | bytes 2359300
  603.1 9.5 %copy-start.4 = (bf16[768,4,128]{0,2,1:T(8,128)(2,1)S(1)}, bf16[768,4,128]{0,2,1:T(8,128)(2,1)}, u32[]{:S(2)}) copy-start(bf16[768,4,128]{0,2,1:T(8,128)(2,1)} %divide_convert_fusion.3) | copy-start | bytes 2359300
  603.1 9.5 %copy-start.5 = (bf16[768,4,128]{0,2,1:T(8,128)(2,1)S(1)}, bf16[768,4,128]{0,2,1:T(8,128)(2,1)}, u32[]{:S(2)}) copy-start(bf16[768,4,128]{0,2,1:T(8,128)(2,1)} %divide_convert_fusion) | copy-start | bytes 2359300
  603.1 9.5 %copy-start.6 = (bf16[768,4,128]{0,2,1:T(8,128)(2,1)S(1)}, bf16[768,4,128]{0,2,1:T(8,128)(2,1)}, u32[]{:S(2)}) copy-start(bf16[768,4,128]{0,2,1:T(8,128)(2,1)} %divide_convert_fusion.1) | copy-start | bytes 2359300
Sparse Core Ops, SparseCore 0:
  11.3 107.6 all-reduce.5
  121.3 42.8 all-gather.1
  484.7 108.7 all-reduce.3
  603.2 17.8 reduce-scatter.1
where the time goes:
time: 634 us; the launch traced here: 629 us
  blocking collectives  297 us (47%)
  waiting for transfers between devices  154 us (24%)
  matrix products  109 us (17%)
  other arithmetic  35.9 us (6%)
  local copies, waits for them, and re-layouts  18.8 us (3%)
  between operations  14.2 us (2%)
    psum x1, blocking collectives, body(): lax.psum((total * factor, mixed * factor[..., None]), 'ctx')  124 us
    pmax x1, blocking collectives, body(): peak = lax.pmax(top, 'ctx')  122 us
    psum x1, waiting for transfers between devices, body(): lax.psum((total * factor, mixed * factor[..., None]), 'ctx')  101 us
    dot_general x8, matrix products, head_stats(): jnp.einsum('rgd,kd->rgk', queries, keys, preferred_element_type=jnp.float32)  62.8 us
    psum x1, waiting for transfers between devices, from_root(): return lax.psum(kept, axis)  49.6 us
    dot_general x8, matrix products, head_stats(): jnp.einsum('rgk,kd->rgd', weights.astype(jnp.bfloat16), values, preferred...  44 us
    all_gather x1, blocking collectives, body(): lax.all_gather(query_k, 'ctx', axis=0, tiled=True)  27.4 us
    all_gather x1, blocking collectives, body(): lax.all_gather(query_v, 'ctx', axis=0, tiled=True)  24 us
  transfers between devices with their start and end apart: 4, of which 3 were waited for; matrix products, arithmetic and copies ran while one was open for 21% of the time, Pallas kernels for 0%

commit v1 on v0

v1 whole, which is shorter than its diff:
```python
import functools
import math

import jax
import jax.numpy as jnp
from jax import lax
from jax.experimental import pallas as pl
from jax.experimental.pallas import tpu as pltpu
from jax.sharding import PartitionSpec as P

HD = 128
SCALE = HD**-0.5 * math.log2(math.e)
F32 = jnp.float32
BF16 = jnp.bfloat16
MESH = pl.DeviceIdType.MESH
CHUNK = 16


def dot(a, b):
    return jnp.dot(a, b, preferred_element_type=F32)


def dot_t(a, b):
    return lax.dot_general(a, b, (((1,), (1,)), ((), ())), preferred_element_type=F32)


def iota(shape, dim):
    return lax.broadcasted_iota(jnp.int32, shape, dim)


def loop(count, step):
    def body(i, carry):
        step(i)
        return carry

    lax.fori_loop(0, count, body, 0)


def kernel(
    nch, ntp, blk,
    ctx_q, ctx_k, ctx_v, query_q, query_k, query_v, weight,
    ctx_out, query_out,
    q_v, k_v, v_v, w_v, pk_v, pv_v, pw_v, out_v,
    vv_own, vv_pair, vv_anchor,
    gq, kvp, an, rs_s, rs_r, lam_v, ag, tp_s, tp_r,
    st_o, st_m,
    sa0, sa1, sa2, pa0, pa1, pa2, sb0, sb1, pb0, pb1, sq0, sq1, pq0, pq1, mq0, mq1,
    loc, pair_s, pair_r, gq_s, gq_r, an_s, an_r, sc_s, pc_r, rs_ss, rs_rs, ag_s, ag_r, tp_ss, tp_rs,
):
    me = lax.axis_index("ctx")
    tp = lax.axis_index("tp")
    chip = me // 2
    core = me % 2
    partner = me + 1 - 2 * core
    tq = blk // 3
    piece = blk // nch

    def local(i, src, dst):
        return pltpu.make_async_copy(src, dst, loc.at[i])

    half = q_v.shape[1] // 2
    lk = local(0, ctx_k, an_view(k_v, nch, piece))
    lv = local(1, ctx_v, an_view(v_v, nch, piece))
    lq0 = local(2, ctx_q.at[:, 0:half], q_v.at[:, 0:half])
    lq1 = local(3, ctx_q.at[:, half:], q_v.at[:, half:])
    lw = local(4, weight, w_v)
    for c in (lk, lv, lq0, lq1, lw):
        c.start()

    barrier = pltpu.get_barrier_semaphore()

    def greet(**where):
        pl.semaphore_signal(barrier, inc=1, device_id=where, device_id_type=MESH)

    loop(nch - 1, lambda i: greet(ctx=2 * ((chip + 1 + i) % nch) + core))
    greet(ctx=partner)

    def greet_tp(i):
        greet(tp=(tp + 1 + i) % ntp)
        greet(tp=(tp + 1 + i) % ntp, ctx=partner)

    loop(ntp - 1, greet_tp)

    @pl.when(me == 0)
    def _():
        loop(nch - 1, lambda i: greet(ctx=2 * (1 + i) + 1))

    @pl.when((core == 1) & (chip > 0))
    def _():
        greet(ctx=0)

    x = query_q[...].astype(F32)
    gq[chip, 0:HD, :] = jnp.concatenate([x[:, h * HD : (h + 1) * HD] for h in range(16)], 0).astype(BF16)
    xk = query_k[...].astype(F32)
    xv = query_v[...].astype(F32)
    gq[chip, HD : HD + 32, :] = jnp.concatenate([xk[:, :HD], xk[:, HD:], xv[:, :HD], xv[:, HD:]], 0).astype(BF16)

    extra = jnp.where(me == 0, nch - 1, jnp.where((core == 1) & (chip > 0), 1, 0))
    pl.semaphore_wait(barrier, nch - 1 + 1 + 2 * (ntp - 1) + extra)

    def remote(src, dst, send, recv, **where):
        return pltpu.make_async_remote_copy(
            src_ref=src, dst_ref=dst, send_sem=send, recv_sem=recv, device_id=where, device_id_type=MESH
        )

    def peer_copy(i, src, dst, send, recv):
        return remote(src, dst, send.at[i], recv.at[chip], ctx=2 * ((chip + 1 + i) % nch) + core)

    def start_peers(src, dst, send, recv):
        loop(nch - 1, lambda i: peer_copy(i, src, dst, send, recv).start())

    def sent_peers(src, dst, send, recv):
        loop(nch - 1, lambda i: peer_copy(i, src, dst, send, recv).wait_send())

    def recv_peers(buf, send, recv):
        def step(i):
            j = (chip + 1 + i) % nch
            remote(buf(j), buf(j), send.at[i], recv.at[j], ctx=2 * j + core).wait_recv()

        loop(nch - 1, step)

    def pair_copy(i, src, dst):
        return remote(src, dst, pair_s.at[i], pair_r.at[i], ctx=partner)

    own_piece = an.at[core, chip]

    def scatter_copies(j):
        ck = remote(ctx_k.at[j], an.at[0, j], sc_s.at[0, j], pc_r.at[0], ctx=2 * j)
        cv = remote(ctx_v.at[j], an.at[1, j], sc_s.at[1, j], pc_r.at[0], ctx=2 * j + 1)
        return ck, cv

    first_key = pltpu.make_async_copy(ctx_k.at[0], an.at[0, 0], pc_r.at[0])

    @pl.when(me == 0)
    def _():
        first_key.start()
        scatter_copies(0)[1].start()

        def step(i):
            ck, cv = scatter_copies(1 + i)
            ck.start()
            cv.start()

        loop(nch - 1, step)

    mine = gq.at[chip]
    start_peers(mine, mine, gq_s, gq_r)
    pk_c = pair_copy(0, ctx_k, an_view(pk_v, nch, piece))
    pv_c = pair_copy(1, ctx_v, an_view(pv_v, nch, piece))
    pk_c.start()
    pv_c.start()

    def fill(vv, v):
        for g in range(2):
            vv[g, :, 0:HD] = v[:, g * HD : (g + 1) * HD]
            vv[g, :, HD:] = jnp.ones((blk, HD), BF16)

    s_a, p_a = (sa0, sa1, sa2), (pa0, pa1, pa2)

    def head_cols(g):
        return pl.ds(pl.multiple_of(g * HD, HD), HD)

    def a_scores(hp, i):
        n = tq * (i + 1)
        q = q_v[i * tq : n, pl.ds(pl.multiple_of(hp * 2 * HD, 2 * HD), 2 * HD)]
        q = jnp.concatenate([q[:, :HD], q[:, HD:]], 0)
        s_a[i][...] = dot_t(q, k_v[0:n, head_cols(hp // 4)])

    def a_soft(hp, i):
        n = tq * (i + 1)
        for r in range(2 * tq // CHUNK):
            low = r * CHUNK
            s = s_a[i][low : low + CHUNK, :]
            keep = iota((CHUNK, tq), 1) <= iota((CHUNK, tq), 0) + low % tq
            d = jnp.where(keep, s[:, n - tq :], -1e30)
            s = d if i == 0 else jnp.concatenate([s[:, : n - tq], d], 1)
            m = jnp.max(s, axis=1, keepdims=True)
            p_a[i][low : low + CHUNK, :] = jnp.exp2((s - m) * SCALE).astype(BF16)
            at = i * tq + low % tq
            st_m[2 * hp + low // tq, at : at + CHUNK, :] = jnp.broadcast_to(m, (CHUNK, HD))

    def a_mix(hp, i):
        n = tq * (i + 1)
        o = dot(p_a[i][...], vv_own[hp // 4, 0:n, :])
        st_o[2 * hp, i * tq : n, :] = o[:tq]
        st_o[2 * hp + 1, i * tq : n, :] = o[tq:]

    def own_block(first, last):
        a_scores(first, 0)

        def step(j):
            hp = first + j
            a_scores(hp, 1)
            a_soft(hp, 0)
            a_mix(hp, 0)
            a_scores(hp, 2)
            a_soft(hp, 1)
            a_mix(hp, 1)
            a_scores(jnp.minimum(hp + 1, last - 1), 0)
            a_soft(hp, 2)
            a_mix(hp, 2)

        loop(last - first, step)

    lk.wait()
    lv.wait()
    fill(vv_own, v_v)
    lq0.wait()
    own_block(0, 2)

    piece_in = remote(own_piece, own_piece, sc_s.at[0, 0], pc_r.at[0], ctx=partner)

    @pl.when(me == 0)
    def _():
        first_key.wait()

    @pl.when(me != 0)
    def _():
        piece_in.wait_recv()

    start_peers(own_piece, own_piece, an_s, an_r)
    own_block(2, 4)

    lq1.wait()
    recv_peers(lambda j: gq.at[j], gq_s, gq_r)
    pk_c.wait_recv()
    pv_c.wait_recv()
    fill(vv_pair, pv_v)
    kv_c = pair_copy(2, gq.at[:, HD : HD + 32, :], kvp)
    kv_c.start()
    w_c = pair_copy(3, weight, pw_v)
    w_c.start()

    s_q, p_q, m_q = (sq0, sq1), (pq0, pq1), (mq0, mq1)
    per_g = nch // 4

    def q_scores(it, b):
        g, t = it // per_g, it % per_g
        q = gq[pl.ds(4 * t, 4), pl.ds(pl.multiple_of(g * 64, 64), 64), :].reshape(256, HD)
        s_q[b][:, 0:blk] = dot_t(q, k_v[:, head_cols(g)])
        s_q[b][:, blk:] = dot_t(q, pk_v[:, head_cols(g)])

    def q_soft(b):
        for r in range(256 // CHUNK):
            rows = slice(r * CHUNK, (r + 1) * CHUNK)
            s = s_q[b][rows, :]
            m = jnp.max(s, axis=1, keepdims=True)
            p_q[b][rows, :] = jnp.exp2((s - m) * SCALE).astype(BF16)
            m_q[b][rows, :] = jnp.broadcast_to(m, (CHUNK, HD))

    def q_mix(it, b):
        g, t = it // per_g, it % per_g
        o = dot(p_q[b][:, 0:blk], vv_own[g]) + dot(p_q[b][:, blk:], vv_pair[g])
        total = o[:, HD:]
        lam = m_q[b][...] * SCALE + jnp.log2(total)
        o = (o[:, :HD] / total).astype(BF16)
        spot = iota((64, HD), 1) - g * 64 == iota((64, HD), 0)
        for u in range(4):
            rs_s[4 * t + u, pl.ds(pl.multiple_of(g * 64, 64), 64), :] = o[u * 64 : (u + 1) * 64]
            row = jnp.sum(jnp.where(spot, lam[u * 64 : (u + 1) * 64], 0.0), axis=0, keepdims=True)
            lam_v[4 * t + u, pl.ds(g, 1), :] = row

    q_scores(0, 0)

    def q_step(j):
        q_scores(2 * j + 1, 1)
        q_soft(0)
        q_mix(2 * j, 0)
        q_scores(jnp.minimum(2 * j + 2, 2 * per_g - 1), 0)
        q_soft(1)
        q_mix(2 * j + 1, 1)

    loop(per_g, q_step)

    def split3(lam):
        hi = lam.astype(BF16).astype(F32)
        mid = (lam - hi).astype(BF16).astype(F32)
        return hi, mid, lam - hi - mid

    hi, mid, low = split3(lam_v[:, 0:1, :] + lam_v[:, 1:2, :])
    row = iota((nch, 16, HD), 1)
    stats = jnp.where(row == 0, hi, jnp.where(row == 1, mid, jnp.where(row == 2, low, 0.0)))
    rs_s[:, HD : HD + 16, :] = stats.astype(BF16)

    def rs_copy(i):
        j = (chip + 1 + i) % nch
        return remote(rs_s.at[j], rs_r.at[chip], rs_ss.at[i], rs_rs.at[chip], ctx=2 * j + core)

    loop(nch - 1, lambda i: rs_copy(i).start())
    rs_r[pl.ds(chip, 1)] = rs_s[pl.ds(chip, 1)]

    own_block(4, 6)
    recv_peers(lambda j: an.at[core, j], an_s, an_r)
    an_c = pair_copy(4, an.at[core], an.at[core])
    an_c.start()
    own_block(6, 8)
    an_c.wait_send()
    remote(an.at[1 - core], an.at[1 - core], pair_s.at[4], pair_r.at[4], ctx=partner).wait_recv()

    for g in range(2):
        vv_anchor[g, :, 0:HD] = an[1, :, :, g * HD : (g + 1) * HD].reshape(blk, HD)
        vv_anchor[g, :, HD:] = jnp.ones((blk, HD), BF16)

    s_b, p_b = (sb0, sb1), (pb0, pb1)

    def b_scores(h, b):
        q = q_v[:, pl.ds(pl.multiple_of(h * HD, HD), HD)]
        keys = an[0, :, :, head_cols(h // 8)].reshape(blk, HD)
        s_b[b][...] = dot_t(q, keys)

    def b_soft(h, b):
        for r in range(blk // CHUNK):
            rows = slice(r * CHUNK, (r + 1) * CHUNK)
            s = s_b[b][rows, :]
            old = st_m[h, rows, :]
            m = jnp.maximum(jnp.max(s, axis=1, keepdims=True), old[:, 0:1])
            p_b[b][rows, :] = jnp.exp2((s - m) * SCALE).astype(BF16)
            st_m[h, rows, :] = jnp.exp2((old - m) * SCALE)

    def b_mix(h, b):
        o = dot(p_b[b][...], vv_anchor[h // 8])
        factor = st_m[h]
        top = factor * st_o[h, :, 0:HD] + o[:, :HD]
        total = factor * st_o[h, :, HD:] + o[:, HD:]
        out_v[:, pl.ds(pl.multiple_of(h * HD, HD), HD)] = (top / total).astype(BF16)

    def anchor_block(first, last):
        @pl.when(me != 0)
        def _():
            b_scores(first, 0)

            def step(j):
                h = first + 2 * j
                b_scores(h + 1, 1)
                b_soft(h, 0)
                b_mix(h, 0)
                b_scores(jnp.minimum(h + 2, last - 1), 0)
                b_soft(h + 1, 1)
                b_mix(h + 1, 1)

            loop((last - first) // 2, step)

        @pl.when(me == 0)
        def _():
            def step(j):
                h = first + j
                value = st_o[h, :, 0:HD] / st_o[h, :, HD:]
                out_v[:, pl.ds(pl.multiple_of(h * HD, HD), HD)] = value.astype(BF16)

            loop(last - first, step)

    anchor_block(0, 8)
    out0 = local(5, out_v.at[:, 0:half], ctx_out.at[:, 0:half])
    out0.start()

    kv_c.wait_recv()

    def self_part():
        kv_own = gq[:, HD : HD + 32, :].astype(F32)
        kv_pair = kvp[...].astype(F32)
        outs, lams = [], []
        count = 16 * nch
        f = iota((64, count), 1)
        second = f // (8 * nch)
        token = (2 * ((f // 8) % nch) + jnp.where(second == 0, core, 1 - core)) * 8 + f % 8
        keep = token <= 8 * me + iota((64, count), 0) % 8
        for g in range(2):
            def pick(first):
                a = kv_own[:, first : first + 8, :].reshape(8 * nch, HD)
                b = kv_pair[:, first : first + 8, :].reshape(8 * nch, HD)
                return jnp.concatenate([a, b], 0).astype(BF16)

            q = gq[chip, g * 64 : (g + 1) * 64, :]
            s = jnp.where(keep, dot_t(q, pick(8 * g)), -1e30)
            m = jnp.max(s, axis=1, keepdims=True)
            p = jnp.exp2((s - m) * SCALE)
            total = jnp.sum(p, axis=1, keepdims=True)
            outs.append((dot(p.astype(BF16), pick(16 + 8 * g)) / total).astype(BF16))
            lam = jnp.broadcast_to(m * SCALE + jnp.log2(total), (64, HD))
            spot = iota((64, HD), 1) - g * 64 == iota((64, HD), 0)
            lams.append(jnp.sum(jnp.where(spot, lam, 0.0), axis=0, keepdims=True))
        return jnp.concatenate(outs, 0), lams[0] + lams[1]

    self_o, self_lam = self_part()
    recv_peers(lambda j: rs_r.at[j], rs_ss, rs_rs)
    stat = rs_r[:, HD : HD + 16, :].astype(F32)
    lam = stat[:, 0, :] + stat[:, 1, :] + stat[:, 2, :]
    peak = jnp.maximum(jnp.max(lam, axis=0, keepdims=True), self_lam)
    share = jnp.exp2(lam - peak)
    self_share = jnp.exp2(self_lam - peak)
    total = jnp.sum(share, axis=0, keepdims=True) + self_share
    eye = iota((HD, HD), 0) == iota((HD, HD), 1)

    def diagonal(v):
        d = jnp.where(eye, jnp.broadcast_to(v, (HD, HD)), 0.0)
        d_hi = d.astype(BF16)
        return jnp.concatenate([d_hi, (d - d_hi.astype(F32)).astype(BF16)], 1)

    acc = dot(diagonal(self_share / total), jnp.concatenate([self_o, self_o], 0))
    share = share / total
    for j in range(nch):
        o = rs_r[j, 0:HD, :]
        acc = acc + dot(diagonal(share[j : j + 1]), jnp.concatenate([o, o], 0))
    ag[pl.ds(chip, 1)] = acc.astype(BF16)[None]
    ag_mine = ag.at[chip]
    start_peers(ag_mine, ag_mine, ag_s, ag_r)

    anchor_block(8, 12)

    recv_peers(lambda j: ag.at[j], ag_s, ag_r)
    w_c.wait_recv()
    lw.wait()
    rows = 8 * nch
    parts = [jnp.zeros((rows, w_v.shape[1]), F32)] * 2
    for hp in range(8):
        both = ag[:, 16 * hp : 16 * hp + 16, :].astype(F32)
        a = jnp.concatenate([both[:, 0:8, :].reshape(rows, HD), both[:, 8:16, :].reshape(rows, HD)], 1).astype(BF16)
        for c, w in enumerate((w_v, pw_v)):
            parts[c] = parts[c] + dot(a, w[hp * 2 * HD : (hp + 1) * 2 * HD, :])
    part = rows // ntp
    for c in range(2):
        for t in range(ntp):
            tp_s[c, t] = parts[c][t * part : (t + 1) * part]

    def tp_copy(i, c):
        t = (tp + 1 + i) % ntp if c == 0 else (tp + i) % ntp
        where = {"tp": t} if c == 0 else {"tp": t, "ctx": partner}
        return remote(tp_s.at[c, t], tp_r.at[c, tp], tp_ss.at[c, i], tp_rs.at[c, tp], **where)

    loop(ntp - 1, lambda i: tp_copy(i, 0).start())
    loop(ntp, lambda i: tp_copy(i, 1).start())

    anchor_block(12, 16)
    out1 = local(6, out_v.at[:, half:], ctx_out.at[:, half:])
    out1.start()

    def tp_recv(c, t):
        buf = tp_r.at[c, t]
        where = {"tp": t} if c == 0 else {"tp": t, "ctx": partner}
        remote(buf, buf, tp_ss.at[c, 0], tp_rs.at[c, t], **where).wait_recv()

    loop(ntp - 1, lambda i: tp_recv(0, (tp + 1 + i) % ntp))
    loop(ntp, lambda i: tp_recv(1, i))
    tp_r[0, pl.ds(tp, 1)] = tp_s[0, pl.ds(tp, 1)]
    mine_sum = jnp.sum(tp_r[0], axis=0)
    pair_sum = jnp.sum(tp_r[1], axis=0)
    groups = part // 8
    even = jnp.where(core == 0, mine_sum, pair_sum).reshape(groups, 1, 8, -1)
    odd = jnp.where(core == 0, pair_sum, mine_sum).reshape(groups, 1, 8, -1)
    query_out[...] = jnp.concatenate([even, odd], 1).reshape(2 * part, -1).astype(BF16)

    sent_peers(mine, mine, gq_s, gq_r)
    sent_peers(own_piece, own_piece, an_s, an_r)
    sent_peers(ag_mine, ag_mine, ag_s, ag_r)
    loop(nch - 1, lambda i: rs_copy(i).wait_send())
    loop(ntp - 1, lambda i: tp_copy(i, 0).wait_send())
    loop(ntp, lambda i: tp_copy(i, 1).wait_send())
    for c in (pk_c, pv_c, kv_c, w_c):
        c.wait_send()

    @pl.when(me == 0)
    def _():
        scatter_copies(0)[1].wait_send()

        def step(i):
            ck, cv = scatter_copies(1 + i)
            ck.wait_send()
            cv.wait_send()

        loop(nch - 1, step)

    out0.wait()
    out1.wait()


def an_view(ref, nch, piece):
    return ref.reshape(nch, piece, ref.shape[-1])


def body(nch, ntp, ctx_q, ctx_k, ctx_v, query_q, query_k, query_v, weight):
    blk, width = ctx_q.shape
    cols = ctx_k.shape[1]
    tq = blk // 3
    piece = blk // nch
    part = 8 * nch // ntp
    vmem = pltpu.VMEM
    dma = pltpu.SemaphoreType.DMA
    scratch = [
        vmem((blk, width), BF16), vmem((blk, cols), BF16), vmem((blk, cols), BF16), vmem(weight.shape, BF16),
        vmem((blk, cols), BF16), vmem((blk, cols), BF16), vmem(weight.shape, BF16), vmem((blk, width), BF16),
        vmem((2, blk, 2 * HD), BF16), vmem((2, blk, 2 * HD), BF16), vmem((2, blk, 2 * HD), BF16),
        vmem((nch, HD + 32, HD), BF16), vmem((nch, 32, HD), BF16), vmem((2, nch, piece, cols), BF16),
        vmem((nch, HD + 16, HD), BF16), vmem((nch, HD + 16, HD), BF16), vmem((nch, 8, HD), F32),
        vmem((nch, HD, HD), BF16), vmem((2, ntp, part, weight.shape[1]), F32), vmem((2, ntp, part, weight.shape[1]), F32),
        vmem((16, blk, 2 * HD), F32), vmem((16, blk, HD), F32),
    ]
    scratch += [vmem((2 * tq, tq * i), F32) for i in (1, 2, 3)] + [vmem((2 * tq, tq * i), BF16) for i in (1, 2, 3)]
    scratch += [vmem((blk, blk), F32)] * 2 + [vmem((blk, blk), BF16)] * 2
    scratch += [vmem((256, 2 * blk), F32)] * 2 + [vmem((256, 2 * blk), BF16)] * 2 + [vmem((256, HD), F32)] * 2
    scratch += [
        dma((7,)), dma((5,)), dma((5,)), dma((nch,)), dma((nch,)), dma((nch,)), dma((nch,)), dma((2, nch)), dma((1,)),
        dma((nch,)), dma((nch,)), dma((nch,)), dma((nch,)), dma((2, ntp)), dma((2, ntp)),
    ]
    hbm = pl.BlockSpec(memory_space=pl.ANY)
    near = pl.BlockSpec(memory_space=pltpu.VMEM)
    return pl.pallas_call(
        functools.partial(kernel, nch, ntp, blk),
        out_shape=(
            jax.ShapeDtypeStruct((blk, width), BF16),
            jax.ShapeDtypeStruct((2 * part, weight.shape[1]), BF16),
        ),
        in_specs=[hbm, hbm, hbm, near, near, near, hbm],
        out_specs=(hbm, near),
        scratch_shapes=scratch,
        compiler_params=pltpu.CompilerParams(
            collective_id=0, has_side_effects=True, vmem_limit_bytes=62 * 2**20
        ),
        name="star",
    )(
        ctx_q, ctx_k.reshape(nch, piece, cols), ctx_v.reshape(nch, piece, cols),
        query_q, query_k, query_v, weight,
    )


def solution(mesh):
    nch, ntp = mesh.shape["ctx"] // 2, mesh.shape["tp"]
    return jax.shard_map(
        functools.partial(body, nch, ntp),
        mesh=mesh,
        in_specs=(P("ctx", "tp"),) * 6 + (P("tp", "ctx"),),
        out_specs=(P("ctx", "tp"), P("tp", "ctx")),
        check_vma=False,
    )
```

time: 634 us -> 68.9 us (0.11)
  blocking collectives: 297 us -> 0 us
  waiting for transfers between devices: 154 us -> 0 us
  matrix products: 109 us -> 0 us
  Pallas kernels: 0 us -> 63.5 us
  other arithmetic: 35.9 us -> 0 us
  local copies, waits for them, and re-layouts: 18.8 us -> 4.59 us
  between operations: 14.2 us -> 0.65 us
    psum x2 -> x0, waiting for transfers between devices: 151 us -> none  [the longest x1 101 us: body(): lax.psum((total * factor, mixed * factor[..., None]), 'ctx')]
    psum x1 -> x0, blocking collectives: 124 us -> none  [body(): lax.psum((total * factor, mixed * factor[..., None]), 'ctx')]
    pmax x1 -> x0, blocking collectives: 122 us -> none  [body(): peak = lax.pmax(top, 'ctx')]
    dot_general x17 -> x0, matrix products: 109 us -> none  [the longest x8 62.8 us: head_stats(): jnp.einsum('rgd,kd->rgk', queries, keys, preferred_element_type=jnp.float32)]
    pallas_call x0 -> x1, Pallas kernels: none -> 63.5 us  [body(): pl.pallas_call(functools.partial(kernel, nch, ntp, blk), out_shape=(jax.S...]
    all_gather x2 -> x0, blocking collectives: 51.5 us -> none  [the longest x1 27.4 us: body(): lax.all_gather(query_k, 'ctx', axis=0, tiled=True)]
    reduce_sum x3 -> x0, other arithmetic: 20.5 us -> none  [head_stats(): total = jnp.sum(weights, axis=2)]
    unnamed x34 -> x4, local copies, waits for them, and re-layouts: 14.1 us -> 4.59 us
  transfers between devices with their start and end apart: 4 -> 0, of which waited for: 3 -> 0; matrix products, arithmetic and copies ran while one was open for 21% -> 0% of each run, Pallas kernels for 0% -> 0%
where the time goes in v1:
time: 68.9 us; the launch traced here: 68.7 us
  Pallas kernels  63.5 us (92%)
  local copies, waits for them, and re-layouts  4.59 us (7%)
    pallas_call x1, Pallas kernels, body(): pl.pallas_call(functools.partial(kernel, nch, ntp, blk), out_shape=(jax.S...  63.5 us
    unnamed x4, local copies, waits for them, and re-layouts  4.59 us

profile of v1, /device:TPU:1, one launch (start us, length us, event | category | flops | bytes accessed | tf_op | source)
XLA Modules:
  0.0 68.7 jit_solution(6959075071616496783)
XLA Ops:
  0.6 63.5 %star.1 = (bf16[768,2048]{1,0:T(8,128)(2,1)}, bf16[64,256]{1,0:T(8,128)(2,1)}) custom-call(bf16[768,2048]{1,0:T(8,128)(2,1)} %ctx_q.1, bf16[16,48,256]{2,1,0:T(8,128)(2,1)} %bitcast.2, bf16[16,48,256]{2,1,0:T(8,128)(2,1)} %bitcast.3, bf16[8,2048]{1,0:T(8,128)(2,1)} %query_q.1, bf16[8,256]{1,0:T(8,128)(2,1)} %query_k.1, bf16[8,256]{1,0:T(8,128)(2,1)} %query_v.1, ...), custom_call_target="tpu_custom_call" | custom-call | tf_op jit(solution)/shard_map/star/pallas_call | solution.py:506
  64.1 0.0 copy-start
  64.1 4.0 %copy.11 = bf16[768,2048]{1,0:T(8,128)(2,1)} copy(bf16[768,2048]{1,0:T(8,128)(2,1)} %get-tuple-element.4) | data formatting | bytes 6291456
  68.1 0.0 copy-done
  68.1 0.6 copy.12
Async XLA Ops:
  64.1 4.0 %copy-start = (bf16[64,256]{1,0:T(8,128)(2,1)S(1)}, bf16[64,256]{1,0:T(8,128)(2,1)}, u32[]{:S(2)}) copy-start(bf16[64,256]{1,0:T(8,128)(2,1)} %get-tuple-element.5) | copy-start | bytes 98308

commit v2 on v1

v2 whole, which is shorter than its diff:
```python
import functools
import math

import jax
import jax.numpy as jnp
from jax import lax
from jax.experimental import pallas as pl
from jax.experimental.pallas import tpu as pltpu
from jax.sharding import PartitionSpec as P

HD = 128
SCALE = HD**-0.5 * math.log2(math.e)
F32 = jnp.float32
BF16 = jnp.bfloat16
MESH = pl.DeviceIdType.MESH
CHUNK = 16


def dot(a, b):
    return jnp.dot(a, b, preferred_element_type=F32)


def dot_t(a, b):
    return lax.dot_general(a, b, (((1,), (1,)), ((), ())), preferred_element_type=F32)


def iota(shape, dim):
    return lax.broadcasted_iota(jnp.int32, shape, dim)


def loop(count, step):
    def body(i, carry):
        step(i)
        return carry

    lax.fori_loop(0, count, body, 0)


def kernel(
    nch, ntp, blk,
    ctx_q, ctx_k, ctx_v, query_q, query_k, query_v, weight,
    ctx_out, query_out,
    q_v, k_v, v_v, w_v, pk_v, pv_v, pw_v, out_v,
    vv_own, vv_pair, vv_anchor,
    qg, kvg, kvp, an, rs_s, rs_r, lam_v, ag, tp_s, tp_r,
    st_o, st_m,
    sa0, sa1, sa2, pa0, pa1, pa2, sb0, sb1, pb0, pb1, sq0, sq1, pq0, pq1, mq0, mq1,
    loc, pair_s, pair_r, ex_s, ex_r, sc_s, pc_r, tp_ss, tp_rs,
):
    me = lax.axis_index("ctx")
    tp = lax.axis_index("tp")
    chip = me // 2
    core = me % 2
    partner = me + 1 - 2 * core
    tq = blk // 3
    piece = blk // nch
    half = q_v.shape[1] // 2

    def local(i, src, dst):
        return pltpu.make_async_copy(src, dst, loc.at[i])

    def half_cols(g):
        return pl.ds(pl.multiple_of(g * HD, HD), HD)

    lk = local(0, ctx_k, an_view(k_v, nch, piece))
    lv = local(1, ctx_v, an_view(v_v, nch, piece))
    lq0 = local(2, ctx_q.at[:, 0:half], q_v.at[:, 0:half])
    lq1 = local(3, ctx_q.at[:, half:], q_v.at[:, half:])
    lw = local(4, weight, w_v)
    out0 = local(5, out_v.at[:, 0:half], ctx_out.at[:, 0:half])
    out1 = local(6, out_v.at[:, half:], ctx_out.at[:, half:])

    def first_key(g):
        return pltpu.make_async_copy(ctx_k.at[0, :, half_cols(g)], an.at[0, g, 0], loc.at[7 + g])

    for c in (lk, lv, lq0, lq1, lw):
        c.start()

    barrier = pltpu.get_barrier_semaphore()

    def greet(**where):
        pl.semaphore_signal(barrier, inc=1, device_id=where, device_id_type=MESH)

    loop(nch - 1, lambda i: greet(ctx=2 * ((chip + 1 + i) % nch) + core))
    greet(ctx=partner)

    def greet_tp(i):
        greet(tp=(tp + 1 + i) % ntp)
        greet(tp=(tp + 1 + i) % ntp, ctx=partner)

    loop(ntp - 1, greet_tp)

    @pl.when(me == 0)
    def _():
        loop(nch - 1, lambda i: greet(ctx=2 * (1 + i) + 1))

    @pl.when((core == 1) & (chip > 0))
    def _():
        greet(ctx=0)

    x = query_q[...].astype(F32)
    for g in range(2):
        rows = [x[:, h * HD : (h + 1) * HD] for h in range(8 * g, 8 * g + 8)]
        qg[g, chip] = jnp.concatenate(rows, 0).astype(BF16)
    xk = query_k[...].astype(F32)
    xv = query_v[...].astype(F32)
    kvg[chip] = jnp.concatenate([xk[:, :HD], xk[:, HD:], xv[:, :HD], xv[:, HD:]], 0).astype(BF16)

    def remote(src, dst, send, recv, **where):
        return pltpu.make_async_remote_copy(
            src_ref=src, dst_ref=dst, send_sem=send, recv_sem=recv, device_id=where, device_id_type=MESH
        )

    def pair_copy(i, src, dst):
        return remote(src, dst, pair_s.at[i], pair_r.at[i], ctx=partner)

    class Spread:
        def __init__(self, index, src, dst):
            self.index, self.src, self.dst = index, src, dst

        def copy(self, i):
            j = (chip + 1 + i) % nch
            send, recv = ex_s.at[self.index, i], ex_r.at[self.index, chip]
            return remote(self.src(j), self.dst(chip), send, recv, ctx=2 * j + core)

        def start(self):
            loop(nch - 1, lambda i: self.copy(i).start())

        def wait_send(self):
            loop(nch - 1, lambda i: self.copy(i).wait_send())

        def wait_recv(self):
            def step(i):
                j = (chip + 1 + i) % nch
                buf = self.dst(j)
                remote(buf, buf, ex_s.at[self.index, i], ex_r.at[self.index, j], ctx=2 * j + core).wait_recv()

            loop(nch - 1, step)

    def queries(g):
        return Spread(g, lambda j: qg.at[g, chip], lambda c: qg.at[g, c])

    def anchors(g):
        return Spread(2 + g, lambda j: an.at[core, g, chip], lambda c: an.at[core, g, c])

    def partials(g):
        return Spread(4 + g, lambda j: rs_s.at[g, j], lambda c: rs_r.at[g, c])

    def merged(g):
        return Spread(6 + g, lambda j: ag.at[g, chip], lambda c: ag.at[g, c])

    query_kv = Spread(8, lambda j: kvg.at[chip], lambda c: kvg.at[c])

    def scatter_copies(g, j):
        ck = remote(ctx_k.at[j, :, half_cols(g)], an.at[0, g, j], sc_s.at[g, 0, j], pc_r.at[g], ctx=2 * j)
        cv = remote(ctx_v.at[j, :, half_cols(g)], an.at[1, g, j], sc_s.at[g, 1, j], pc_r.at[g], ctx=2 * j + 1)
        return ck, cv

    def scatter(g):
        @pl.when(me == 0)
        def _():
            first_key(g).start()
            scatter_copies(g, 0)[1].start()

            def step(i):
                ck, cv = scatter_copies(g, 1 + i)
                ck.start()
                cv.start()

            loop(nch - 1, step)

    pk_c = pair_copy(0, ctx_k, an_view(pk_v, nch, piece))
    pv_c = pair_copy(1, ctx_v, an_view(pv_v, nch, piece))
    kv_c = pair_copy(2, kvg, kvp)
    w_c = pair_copy(3, weight, pw_v)

    def anchor_pair(g):
        return pair_copy(4 + g, an.at[core, g], an.at[core, g])

    def begin():
        extra = jnp.where(me == 0, nch - 1, jnp.where((core == 1) & (chip > 0), 1, 0))
        pl.semaphore_wait(barrier, nch - 1 + 1 + 2 * (ntp - 1) + extra)
        scatter(0)
        queries(0).start()
        pk_c.start()
        pv_c.start()
        scatter(1)
        queries(1).start()
        query_kv.start()

    def hand_on(g):
        @pl.when(me == 0)
        def _():
            first_key(g).wait()

        @pl.when(me != 0)
        def _():
            own = an.at[core, g, chip]
            remote(own, own, sc_s.at[g, 0, 0], pc_r.at[g], ctx=partner).wait_recv()

        anchors(g).start()

    def fill(vv, v):
        for g in range(2):
            vv[g, :, 0:HD] = v[:, g * HD : (g + 1) * HD]
            vv[g, :, HD:] = jnp.ones((blk, HD), BF16)

    s_a, p_a = (sa0, sa1, sa2), (pa0, pa1, pa2)

    def a_scores(hp, i):
        n = tq * (i + 1)
        q = q_v[i * tq : n, pl.ds(pl.multiple_of(hp * 2 * HD, 2 * HD), 2 * HD)]
        q = jnp.concatenate([q[:, :HD], q[:, HD:]], 0)
        s_a[i][...] = dot_t(q, k_v[0:n, half_cols(hp // 4)])

    def a_soft(hp, i):
        n = tq * (i + 1)
        for r in range(2 * tq // CHUNK):
            low = r * CHUNK
            s = s_a[i][low : low + CHUNK, :]
            keep = iota((CHUNK, tq), 1) <= iota((CHUNK, tq), 0) + low % tq
            d = jnp.where(keep, s[:, n - tq :], -1e30)
            s = d if i == 0 else jnp.concatenate([s[:, : n - tq], d], 1)
            m = jnp.max(s, axis=1, keepdims=True)
            p_a[i][low : low + CHUNK, :] = jnp.exp2((s - m) * SCALE).astype(BF16)
            at = i * tq + low % tq
            st_m[2 * hp + low // tq, at : at + CHUNK, :] = jnp.broadcast_to(m, (CHUNK, HD))

    def a_mix(hp, i):
        n = tq * (i + 1)
        o = dot(p_a[i][...], vv_own[hp // 4, 0:n, :])
        st_o[2 * hp, i * tq : n, :] = o[:tq]
        st_o[2 * hp + 1, i * tq : n, :] = o[tq:]

    s_q, p_q, m_q = (sq0, sq1), (pq0, pq1), (mq0, mq1)
    per_g = nch // 4

    def q_scores(g, t, b):
        q = qg[g, pl.ds(4 * t, 4)].reshape(256, HD)
        s_q[b][:, 0:blk] = dot_t(q, k_v[:, half_cols(g)])
        s_q[b][:, blk:] = dot_t(q, pk_v[:, half_cols(g)])

    def q_soft(b):
        for r in range(256 // CHUNK):
            rows = slice(r * CHUNK, (r + 1) * CHUNK)
            s = s_q[b][rows, :]
            m = jnp.max(s, axis=1, keepdims=True)
            p_q[b][rows, :] = jnp.exp2((s - m) * SCALE).astype(BF16)
            m_q[b][rows, :] = jnp.broadcast_to(m, (CHUNK, HD))

    twice = iota((64, HD), 1) % 64 == iota((64, HD), 0)
    first = iota((1, HD), 1) < 64

    def as_row(column):
        return jnp.sum(jnp.where(twice, column, 0.0), axis=0, keepdims=True)

    def q_mix(g, t, b):
        o = dot(p_q[b][:, 0:blk], vv_own[g]) + dot(p_q[b][:, blk:], vv_pair[g])
        total = o[:, HD:]
        lam = m_q[b][...] * SCALE + jnp.log2(total)
        o = (o[:, :HD] / total).astype(BF16)
        for u in range(4):
            rs_s[g, 4 * t + u, 0:64, :] = o[u * 64 : (u + 1) * 64]
            lam_v[4 * t + u, 0:1, :] = as_row(lam[u * 64 : (u + 1) * 64])

    def query_half(g):
        queries(g).wait_recv()

        @pl.when(g == 0)
        def _():
            pk_c.wait_recv()
            pv_c.wait_recv()
            fill(vv_pair, pv_v)

        q_scores(g, 0, 0)

        def step(j):
            q_scores(g, 2 * j + 1, 1)
            q_soft(0)
            q_mix(g, 2 * j, 0)
            q_scores(g, jnp.minimum(2 * j + 2, per_g - 1), 0)
            q_soft(1)
            q_mix(g, 2 * j + 1, 1)

        loop(per_g // 2, step)
        lam = lam_v[:, 0:1, :]
        hi = lam.astype(BF16).astype(F32)
        mid = (lam - hi).astype(BF16).astype(F32)
        row = iota((nch, 16, HD), 1)
        stats = jnp.where(row == 0, hi, jnp.where(row == 1, mid, jnp.where(row == 2, lam - hi - mid, 0.0)))
        rs_s[g, :, 64:80, :] = stats.astype(BF16)
        partials(g).start()
        rs_r[g, pl.ds(chip, 1)] = rs_s[g, pl.ds(chip, 1)]

    def anchors_across(g):
        anchors(g).wait_recv()
        anchor_pair(g).start()

    early = (114 - 7 * tp - 9 * (chip // 4) - 18 * (chip % 4)) // 28
    early = jnp.maximum(0, jnp.minimum(4, early))
    at_piece = jnp.maximum(2, early + 1)
    at_query = jnp.maximum(4, at_piece + 1)

    lk.wait()
    lv.wait()
    fill(vv_own, v_v)
    lq0.wait()
    a_scores(0, 0)

    def own_step(j):
        @pl.when(j > 0)
        def _():
            hp = j - 1
            a_scores(hp, 1)
            a_soft(hp, 0)
            a_mix(hp, 0)
            a_scores(hp, 2)
            a_soft(hp, 1)
            a_mix(hp, 1)
            a_scores(jnp.minimum(hp + 1, 7), 0)
            a_soft(hp, 2)
            a_mix(hp, 2)

        pl.when(j == 3)(lq1.wait)
        pl.when(j == early)(begin)
        pl.when(j == at_piece)(lambda: hand_on(0))
        pl.when(j == at_piece + 1)(lambda: hand_on(1))

        @pl.when(j == at_query)
        def _():
            loop(2, query_half)
            query_kv.wait_recv()
            anchors_across(0)
            anchors_across(1)
            kv_c.start()
            w_c.start()

    loop(9, own_step)

    s_b, p_b = (sb0, sb1), (pb0, pb1)

    def b_scores(h, b):
        q = q_v[:, pl.ds(pl.multiple_of(h * HD, HD), HD)]
        s_b[b][...] = dot_t(q, an[0, h // 8].reshape(blk, HD))

    def b_soft(h, b):
        for r in range(blk // CHUNK):
            rows = slice(r * CHUNK, (r + 1) * CHUNK)
            s = s_b[b][rows, :]
            old = st_m[h, rows, :]
            m = jnp.maximum(jnp.max(s, axis=1, keepdims=True), old[:, 0:1])
            p_b[b][rows, :] = jnp.exp2((s - m) * SCALE).astype(BF16)
            st_m[h, rows, :] = jnp.exp2((old - m) * SCALE)

    def b_mix(h, b):
        o = dot(p_b[b][...], vv_anchor[h // 8])
        factor = st_m[h]
        top = factor * st_o[h, :, 0:HD] + o[:, :HD]
        total = factor * st_o[h, :, HD:] + o[:, HD:]
        out_v[:, pl.ds(pl.multiple_of(h * HD, HD), HD)] = (top / total).astype(BF16)

    def anchor_in(g):
        other = an.at[1 - core, g]
        remote(other, other, pair_s.at[4 + g], pair_r.at[4 + g], ctx=partner).wait_recv()
        vv_anchor[g, :, 0:HD] = an[1, g].reshape(blk, HD)
        vv_anchor[g, :, HD:] = jnp.ones((blk, HD), BF16)

    def self_half(g):
        count = 16 * nch
        f = iota((64, count), 1)
        side = jnp.where(f // (8 * nch) == 0, core, 1 - core)
        token = (2 * ((f // 8) % nch) + side) * 8 + f % 8
        keep = token <= 8 * me + iota((64, count), 0) % 8

        def pick(at):
            own = kvg[:, 16 * at : 16 * at + 16, :].astype(F32)
            pair = kvp[:, 16 * at : 16 * at + 16, :].astype(F32)
            both = [
                jnp.where(g == 0, a[:, 0:8, :], a[:, 8:16, :]).reshape(8 * nch, HD) for a in (own, pair)
            ]
            return jnp.concatenate(both, 0).astype(BF16)

        s = jnp.where(keep, dot_t(qg[g, chip], pick(0)), -1e30)
        m = jnp.max(s, axis=1, keepdims=True)
        p = jnp.exp2((s - m) * SCALE)
        total = jnp.sum(p, axis=1, keepdims=True)
        lam = jnp.broadcast_to(m * SCALE + jnp.log2(total), (64, HD))
        return dot(p.astype(BF16), pick(1)) / total, as_row(lam)

    def spot(share):
        hi = share.astype(BF16).astype(F32)
        return jnp.where(twice, jnp.where(first, hi, share - hi), 0.0).astype(BF16)

    def merge_half(g):
        own, own_lam = self_half(g)
        partials(g).wait_recv()
        stat = rs_r[g, :, 64:80, :].astype(F32)
        lam = stat[:, 0, :] + stat[:, 1, :] + stat[:, 2, :]
        peak = jnp.maximum(jnp.max(lam, axis=0, keepdims=True), own_lam)
        share = jnp.exp2(lam - peak)
        own_share = jnp.exp2(own_lam - peak)
        total = jnp.sum(share, axis=0, keepdims=True) + own_share
        share = share / total
        own = own.astype(BF16)
        acc = dot(spot(own_share / total), jnp.concatenate([own, own], 0))
        for j in range(0, nch, 2):
            left = jnp.concatenate([spot(share[j : j + 1]), spot(share[j + 1 : j + 2])], 1)
            a, b = rs_r[g, j, 0:64, :], rs_r[g, j + 1, 0:64, :]
            acc = acc + dot(left, jnp.concatenate([a, a, b, b], 0))
        ag[g, pl.ds(chip, 1)] = acc.astype(BF16)[None]
        merged(g).start()

    rows = 8 * nch
    part = rows // ntp

    def tp_copy(i, c):
        t = (tp + 1 + i) % ntp if c == 0 else (tp + i) % ntp
        where = {"tp": t} if c == 0 else {"tp": t, "ctx": partner}
        return remote(tp_s.at[c, t], tp_r.at[c, tp], tp_ss.at[c, i], tp_rs.at[c, tp], **where)

    def project():
        merged(0).wait_recv()
        merged(1).wait_recv()
        w_c.wait_recv()
        lw.wait()
        parts = [jnp.zeros((rows, w_v.shape[1]), F32)] * 2
        for hp in range(8):
            both = ag[hp // 4, :, 16 * (hp % 4) : 16 * (hp % 4) + 16, :].astype(F32)
            a = jnp.concatenate([both[:, 0:8, :].reshape(rows, HD), both[:, 8:16, :].reshape(rows, HD)], 1)
            for c, w in enumerate((w_v, pw_v)):
                parts[c] = parts[c] + dot(a.astype(BF16), w[hp * 2 * HD : (hp + 1) * 2 * HD, :])
        for c in range(2):
            for t in range(ntp):
                tp_s[c, t] = parts[c][t * part : (t + 1) * part].astype(BF16)
        loop(ntp - 1, lambda i: tp_copy(i, 0).start())
        loop(ntp, lambda i: tp_copy(i, 1).start())

    def anchor_step(j):
        pl.when(j == 1)(lambda: merge_half(0))
        pl.when(j == 2)(lambda: merge_half(1))
        pl.when(j == 3)(lambda: anchor_in(1))
        pl.when(j == 4)(out0.start)
        pl.when(j == 5)(project)
        h = 2 * j

        @pl.when(me != 0)
        def _():
            b_scores(h + 1, 1)
            b_soft(h, 0)
            b_mix(h, 0)
            b_scores(jnp.minimum(h + 2, 15), 0)
            b_soft(h + 1, 1)
            b_mix(h + 1, 1)

        @pl.when(me == 0)
        def _():
            for k in (h, h + 1):
                value = st_o[k, :, 0:HD] / st_o[k, :, HD:]
                out_v[:, pl.ds(pl.multiple_of(k * HD, HD), HD)] = value.astype(BF16)

    kv_c.wait_recv()
    anchor_in(0)
    b_scores(0, 0)
    loop(8, anchor_step)
    out1.start()

    def tp_recv(c, t):
        buf = tp_r.at[c, t]
        where = {"tp": t} if c == 0 else {"tp": t, "ctx": partner}
        remote(buf, buf, tp_ss.at[c, 0], tp_rs.at[c, t], **where).wait_recv()

    loop(ntp - 1, lambda i: tp_recv(0, (tp + 1 + i) % ntp))
    loop(ntp, lambda i: tp_recv(1, i))
    tp_r[0, pl.ds(tp, 1)] = tp_s[0, pl.ds(tp, 1)]
    mine_sum = jnp.sum(tp_r[0].astype(F32), axis=0)
    pair_sum = jnp.sum(tp_r[1].astype(F32), axis=0)
    groups = part // 8
    even = jnp.where(core == 0, mine_sum, pair_sum).reshape(groups, 1, 8, -1)
    odd = jnp.where(core == 0, pair_sum, mine_sum).reshape(groups, 1, 8, -1)
    query_out[...] = jnp.concatenate([even, odd], 1).reshape(2 * part, -1).astype(BF16)

    def sent(g):
        for spread in (queries(g), anchors(g), partials(g), merged(g)):
            spread.wait_send()
        anchor_pair(g).wait_send()

        @pl.when(me == 0)
        def _():
            scatter_copies(g, 0)[1].wait_send()

            def step(i):
                ck, cv = scatter_copies(g, 1 + i)
                ck.wait_send()
                cv.wait_send()

            loop(nch - 1, step)

    loop(2, sent)
    query_kv.wait_send()
    loop(ntp - 1, lambda i: tp_copy(i, 0).wait_send())
    loop(ntp, lambda i: tp_copy(i, 1).wait_send())
    for c in (pk_c, pv_c, kv_c, w_c):
        c.wait_send()
    out0.wait()
    out1.wait()


def an_view(ref, nch, piece):
    return ref.reshape(nch, piece, ref.shape[-1])


def body(nch, ntp, ctx_q, ctx_k, ctx_v, query_q, query_k, query_v, weight):
    blk, width = ctx_q.shape
    cols = ctx_k.shape[1]
    tq = blk // 3
    piece = blk // nch
    part = 8 * nch // ntp
    vmem = pltpu.VMEM
    dma = pltpu.SemaphoreType.DMA
    scratch = [
        vmem((blk, width), BF16), vmem((blk, cols), BF16), vmem((blk, cols), BF16), vmem(weight.shape, BF16),
        vmem((blk, cols), BF16), vmem((blk, cols), BF16), vmem(weight.shape, BF16), vmem((blk, width), BF16),
        vmem((2, blk, 2 * HD), BF16), vmem((2, blk, 2 * HD), BF16), vmem((2, blk, 2 * HD), BF16),
        vmem((2, nch, 64, HD), BF16), vmem((nch, 32, HD), BF16), vmem((nch, 32, HD), BF16),
        vmem((2, 2, nch, piece, HD), BF16),
        vmem((2, nch, 80, HD), BF16), vmem((2, nch, 80, HD), BF16), vmem((nch, 8, HD), F32),
        vmem((2, nch, 64, HD), BF16), vmem((2, ntp, part, weight.shape[1]), BF16), vmem((2, ntp, part, weight.shape[1]), BF16),
        vmem((16, blk, 2 * HD), F32), vmem((16, blk, HD), F32),
    ]
    scratch += [vmem((2 * tq, tq * i), F32) for i in (1, 2, 3)] + [vmem((2 * tq, tq * i), BF16) for i in (1, 2, 3)]
    scratch += [vmem((blk, blk), F32)] * 2 + [vmem((blk, blk), BF16)] * 2
    scratch += [vmem((256, 2 * blk), F32)] * 2 + [vmem((256, 2 * blk), BF16)] * 2 + [vmem((256, HD), F32)] * 2
    scratch += [
        dma((9,)), dma((6,)), dma((6,)), dma((9, nch)), dma((9, nch)), dma((2, 2, nch)), dma((2,)),
        dma((2, ntp)), dma((2, ntp)),
    ]
    hbm = pl.BlockSpec(memory_space=pl.ANY)
    near = pl.BlockSpec(memory_space=pltpu.VMEM)
    return pl.pallas_call(
        functools.partial(kernel, nch, ntp, blk),
        out_shape=(
            jax.ShapeDtypeStruct((blk, width), BF16),
            jax.ShapeDtypeStruct((2 * part, weight.shape[1]), BF16),
        ),
        in_specs=[hbm, hbm, hbm, near, near, near, hbm],
        out_specs=(hbm, near),
        scratch_shapes=scratch,
        compiler_params=pltpu.CompilerParams(
            collective_id=0, has_side_effects=True, vmem_limit_bytes=62 * 2**20
        ),
        name="star",
    )(
        ctx_q, ctx_k.reshape(nch, piece, cols), ctx_v.reshape(nch, piece, cols),
        query_q, query_k, query_v, weight,
    )


def solution(mesh):
    nch, ntp = mesh.shape["ctx"] // 2, mesh.shape["tp"]
    return jax.shard_map(
        functools.partial(body, nch, ntp),
        mesh=mesh,
        in_specs=(P("ctx", "tp"),) * 6 + (P("tp", "ctx"),),
        out_specs=(P("ctx", "tp"), P("tp", "ctx")),
        check_vma=False,
    )
```

time: 68.9 us -> 66.2 us (0.961)
  Pallas kernels: 63.5 us -> 60.7 us
    pallas_call x1, Pallas kernels: 63.5 us -> 60.7 us  [body(): pl.pallas_call(functools.partial(kernel, nch, ntp, blk), out_shape=(jax.S...]
where the time goes in v2:
time: 66.2 us; the launch traced here: 66 us
  Pallas kernels  60.7 us (92%)
  local copies, waits for them, and re-layouts  4.59 us (7%)
    pallas_call x1, Pallas kernels, body(): pl.pallas_call(functools.partial(kernel, nch, ntp, blk), out_shape=(jax.S...  60.7 us
    unnamed x4, local copies, waits for them, and re-layouts  4.59 us

profile of v2, /device:TPU:1, one launch (start us, length us, event | category | flops | bytes accessed | tf_op | source)
XLA Modules:
  0.0 66.0 jit_solution(14168846270557528061)
XLA Ops:
  0.6 60.7 %star.1 = (bf16[768,2048]{1,0:T(8,128)(2,1)}, bf16[64,256]{1,0:T(8,128)(2,1)}) custom-call(bf16[768,2048]{1,0:T(8,128)(2,1)} %ctx_q.1, bf16[16,48,256]{2,1,0:T(8,128)(2,1)} %bitcast.2, bf16[16,48,256]{2,1,0:T(8,128)(2,1)} %bitcast.3, bf16[8,2048]{1,0:T(8,128)(2,1)} %query_q.1, bf16[8,256]{1,0:T(8,128)(2,1)} %query_k.1, bf16[8,256]{1,0:T(8,128)(2,1)} %query_v.1, ...), custom_call_target="tpu_custom_call" | custom-call | tf_op jit(solution)/shard_map/star/pallas_call | solution.py:539
  61.4 0.0 copy-start
  61.4 4.0 %copy.11 = bf16[768,2048]{1,0:T(8,128)(2,1)} copy(bf16[768,2048]{1,0:T(8,128)(2,1)} %get-tuple-element.4) | data formatting | bytes 6291456
  65.3 0.0 copy-done
  65.3 0.6 copy.12
Async XLA Ops:
  61.4 4.0 %copy-start = (bf16[64,256]{1,0:T(8,128)(2,1)S(1)}, bf16[64,256]{1,0:T(8,128)(2,1)}, u32[]{:S(2)}) copy-start(bf16[64,256]{1,0:T(8,128)(2,1)} %get-tuple-element.5) | copy-start | bytes 98308

commit v3 on v2

--- a/solution.py
+++ b/solution.py
@@ -54,7 +54,6 @@
     partner = me + 1 - 2 * core
     tq = blk // 3
     piece = blk // nch
-    half = q_v.shape[1] // 2
 
     def local(i, src, dst):
         return pltpu.make_async_copy(src, dst, loc.at[i])
@@ -64,17 +63,23 @@
 
     lk = local(0, ctx_k, an_view(k_v, nch, piece))
     lv = local(1, ctx_v, an_view(v_v, nch, piece))
-    lq0 = local(2, ctx_q.at[:, 0:half], q_v.at[:, 0:half])
-    lq1 = local(3, ctx_q.at[:, half:], q_v.at[:, half:])
-    lw = local(4, weight, w_v)
-    out0 = local(5, out_v.at[:, 0:half], ctx_out.at[:, 0:half])
-    out1 = local(6, out_v.at[:, half:], ctx_out.at[:, half:])
+    lw = local(2, weight, w_v)
+
+    def strip(i):
+        return pl.ds(pl.multiple_of(i * 2 * HD, 2 * HD), 2 * HD)
+
+    def queries_in(i):
+        return local(5 + i, ctx_q.at[:, strip(i)], q_v.at[:, strip(i)])
+
+    def result_out(i):
+        return local(13 + i, out_v.at[:, strip(i)], ctx_out.at[:, strip(i)])
 
     def first_key(g):
-        return pltpu.make_async_copy(ctx_k.at[0, :, half_cols(g)], an.at[0, g, 0], loc.at[7 + g])
-
-    for c in (lk, lv, lq0, lq1, lw):
-        c.start()
+        return pltpu.make_async_copy(ctx_k.at[0, :, half_cols(g)], an.at[0, g, 0], loc.at[3 + g])
+
+    lk.start()
+    lv.start()
+    loop(8, lambda i: queries_in(i).start())
 
     barrier = pltpu.get_barrier_semaphore()
 
@@ -180,12 +185,12 @@
     def begin():
         extra = jnp.where(me == 0, nch - 1, jnp.where((core == 1) & (chip > 0), 1, 0))
         pl.semaphore_wait(barrier, nch - 1 + 1 + 2 * (ntp - 1) + extra)
+        queries(0).start()
         scatter(0)
-        queries(0).start()
         pk_c.start()
         pv_c.start()
+        queries(1).start()
         scatter(1)
-        queries(1).start()
         query_kv.start()
 
     def hand_on(g):
@@ -290,6 +295,7 @@
         stats = jnp.where(row == 0, hi, jnp.where(row == 1, mid, jnp.where(row == 2, lam - hi - mid, 0.0)))
         rs_s[g, :, 64:80, :] = stats.astype(BF16)
         partials(g).start()
+        hand_on(g)
         rs_r[g, pl.ds(chip, 1)] = rs_s[g, pl.ds(chip, 1)]
 
     def anchors_across(g):
@@ -298,16 +304,19 @@
 
     early = (114 - 7 * tp - 9 * (chip // 4) - 18 * (chip % 4)) // 28
     early = jnp.maximum(0, jnp.minimum(4, early))
-    at_piece = jnp.maximum(2, early + 1)
-    at_query = jnp.maximum(4, at_piece + 1)
+    at_query = jnp.maximum(4, early + 1)
 
     lk.wait()
     lv.wait()
     fill(vv_own, v_v)
-    lq0.wait()
+    queries_in(0).wait()
     a_scores(0, 0)
 
     def own_step(j):
+        @pl.when((j > 0) & (j < 8))
+        def _():
+            queries_in(j).wait()
+
         @pl.when(j > 0)
         def _():
             hp = j - 1
@@ -321,19 +330,16 @@
             a_soft(hp, 2)
             a_mix(hp, 2)
 
-        pl.when(j == 3)(lq1.wait)
         pl.when(j == early)(begin)
-        pl.when(j == at_piece)(lambda: hand_on(0))
-        pl.when(j == at_piece + 1)(lambda: hand_on(1))
-
         @pl.when(j == at_query)
         def _():
             loop(2, query_half)
             query_kv.wait_recv()
-            anchors_across(0)
-            anchors_across(1)
             kv_c.start()
             w_c.start()
+            lw.start()
+
+        pl.when(j == 7)(lambda: anchors_across(0))
 
     loop(9, own_step)
 
@@ -436,11 +442,15 @@
         loop(ntp, lambda i: tp_copy(i, 1).start())
 
     def anchor_step(j):
-        pl.when(j == 1)(lambda: merge_half(0))
-        pl.when(j == 2)(lambda: merge_half(1))
+        @pl.when(j == 0)
+        def _():
+            kv_c.wait_recv()
+            merge_half(0)
+
+        pl.when(j == 1)(lambda: merge_half(1))
+        pl.when(j == 1)(lambda: anchors_across(1))
         pl.when(j == 3)(lambda: anchor_in(1))
-        pl.when(j == 4)(out0.start)
-        pl.when(j == 5)(project)
+        pl.when(j == 4)(project)
         h = 2 * j
 
         @pl.when(me != 0)
@@ -458,11 +468,11 @@
                 value = st_o[k, :, 0:HD] / st_o[k, :, HD:]
                 out_v[:, pl.ds(pl.multiple_of(k * HD, HD), HD)] = value.astype(BF16)
 
-    kv_c.wait_recv()
+        result_out(j).start()
+
     anchor_in(0)
     b_scores(0, 0)
     loop(8, anchor_step)
-    out1.start()
 
     def tp_recv(c, t):
         buf = tp_r.at[c, t]
@@ -501,8 +511,7 @@
     loop(ntp, lambda i: tp_copy(i, 1).wait_send())
     for c in (pk_c, pv_c, kv_c, w_c):
         c.wait_send()
-    out0.wait()
-    out1.wait()
+    loop(8, lambda i: result_out(i).wait())
 
 
 def an_view(ref, nch, piece):
@@ -531,7 +540,7 @@
     scratch += [vmem((blk, blk), F32)] * 2 + [vmem((blk, blk), BF16)] * 2
     scratch += [vmem((256, 2 * blk), F32)] * 2 + [vmem((256, 2 * blk), BF16)] * 2 + [vmem((256, HD), F32)] * 2
     scratch += [
-        dma((9,)), dma((6,)), dma((6,)), dma((9, nch)), dma((9, nch)), dma((2, 2, nch)), dma((2,)),
+        dma((21,)), dma((6,)), dma((6,)), dma((9, nch)), dma((9, nch)), dma((2, 2, nch)), dma((2,)),
         dma((2, ntp)), dma((2, ntp)),
     ]
     hbm = pl.BlockSpec(memory_space=pl.ANY)

time: 66.2 us -> 60.3 us (0.911)
  Pallas kernels: 60.7 us -> 54.8 us
    pallas_call x1, Pallas kernels: 60.7 us -> 54.8 us  [body(): pl.pallas_call(functools.partial(kernel, nch, ntp, blk), out_shape=(jax.S...]
where the time goes in v3:
time: 60.3 us; the launch traced here: 60 us
  Pallas kernels  54.8 us (91%)
  local copies, waits for them, and re-layouts  4.59 us (8%)
  between operations  0.65 us (1%)
    pallas_call x1, Pallas kernels, body(): pl.pallas_call(functools.partial(kernel, nch, ntp, blk), out_shape=(jax.S...  54.8 us
    unnamed x4, local copies, waits for them, and re-layouts  4.59 us

profile of v3, /device:TPU:1, one launch (start us, length us, event | category | flops | bytes accessed | tf_op | source)
XLA Modules:
  0.0 60.0 jit_solution(17297578037157006346)
XLA Ops:
  0.6 54.8 %star.1 = (bf16[768,2048]{1,0:T(8,128)(2,1)}, bf16[64,256]{1,0:T(8,128)(2,1)}) custom-call(bf16[768,2048]{1,0:T(8,128)(2,1)} %ctx_q.1, bf16[16,48,256]{2,1,0:T(8,128)(2,1)} %bitcast.2, bf16[16,48,256]{2,1,0:T(8,128)(2,1)} %bitcast.3, bf16[8,2048]{1,0:T(8,128)(2,1)} %query_q.1, bf16[8,256]{1,0:T(8,128)(2,1)} %query_k.1, bf16[8,256]{1,0:T(8,128)(2,1)} %query_v.1, ...), custom_call_target="tpu_custom_call" | custom-call | tf_op jit(solution)/shard_map/star/pallas_call | solution.py:548
  55.4 0.0 copy-start
  55.4 4.0 %copy.11 = bf16[768,2048]{1,0:T(8,128)(2,1)} copy(bf16[768,2048]{1,0:T(8,128)(2,1)} %get-tuple-element.4) | data formatting | bytes 6291456
  59.4 0.0 copy-done
  59.4 0.6 %copy.12 = bf16[64,256]{1,0:T(8,128)(2,1)} copy(bf16[64,256]{1,0:T(8,128)(2,1)S(1)} %copy-done) | data formatting | bytes 65536
Async XLA Ops:
  55.4 4.0 %copy-start = (bf16[64,256]{1,0:T(8,128)(2,1)S(1)}, bf16[64,256]{1,0:T(8,128)(2,1)}, u32[]{:S(2)}) copy-start(bf16[64,256]{1,0:T(8,128)(2,1)} %get-tuple-element.5) | copy-start | bytes 98308

commit v4 on v3

--- a/solution.py
+++ b/solution.py
@@ -295,17 +295,18 @@
         stats = jnp.where(row == 0, hi, jnp.where(row == 1, mid, jnp.where(row == 2, lam - hi - mid, 0.0)))
         rs_s[g, :, 64:80, :] = stats.astype(BF16)
         partials(g).start()
-        hand_on(g)
+        pl.when(g == 0)(lambda: hand_on(0))
         rs_r[g, pl.ds(chip, 1)] = rs_s[g, pl.ds(chip, 1)]
 
     def anchors_across(g):
         anchors(g).wait_recv()
         anchor_pair(g).start()
 
-    early = (114 - 7 * tp - 9 * (chip // 4) - 18 * (chip % 4)) // 28
+    early = (86 - 7 * tp - 9 * (chip // 4) - 18 * (chip % 4)) // 28
     early = jnp.maximum(0, jnp.minimum(4, early))
     at_query = jnp.maximum(4, early + 1)
 
+    pl.when(early == 0)(begin)
     lk.wait()
     lv.wait()
     fill(vv_own, v_v)
@@ -330,7 +331,7 @@
             a_soft(hp, 2)
             a_mix(hp, 2)
 
-        pl.when(j == early)(begin)
+        pl.when((j == early) & (j > 0))(begin)
         @pl.when(j == at_query)
         def _():
             loop(2, query_half)
@@ -339,6 +340,7 @@
             w_c.start()
             lw.start()
 
+        pl.when(j == at_query + 2)(lambda: hand_on(1))
         pl.when(j == 7)(lambda: anchors_across(0))
 
     loop(9, own_step)
@@ -448,7 +450,7 @@
             merge_half(0)
 
         pl.when(j == 1)(lambda: merge_half(1))
-        pl.when(j == 1)(lambda: anchors_across(1))
+        pl.when(j == 2)(lambda: anchors_across(1))
         pl.when(j == 3)(lambda: anchor_in(1))
         pl.when(j == 4)(project)
         h = 2 * j

time: 60.3 us -> 60.7 us (level)
  no operation moved by 1% of the time
where the time goes in v4:
time: 60.7 us; the launch traced here: 60.2 us
  Pallas kernels  54.9 us (90%)
  local copies, waits for them, and re-layouts  4.59 us (8%)
  between operations  0.65 us (1%)
    pallas_call x1, Pallas kernels, body(): pl.pallas_call(functools.partial(kernel, nch, ntp, blk), out_shape=(jax.S...  54.9 us
    unnamed x4, local copies, waits for them, and re-layouts  4.59 us

profile of v4, /device:TPU:1, one launch (start us, length us, event | category | flops | bytes accessed | tf_op | source)
XLA Modules:
  0.0 60.2 jit_solution(10782319810691442357)
XLA Ops:
  0.6 54.9 %star.1 = (bf16[768,2048]{1,0:T(8,128)(2,1)}, bf16[64,256]{1,0:T(8,128)(2,1)}) custom-call(bf16[768,2048]{1,0:T(8,128)(2,1)} %ctx_q.1, bf16[16,48,256]{2,1,0:T(8,128)(2,1)} %bitcast.2, bf16[16,48,256]{2,1,0:T(8,128)(2,1)} %bitcast.3, bf16[8,2048]{1,0:T(8,128)(2,1)} %query_q.1, bf16[8,256]{1,0:T(8,128)(2,1)} %query_k.1, bf16[8,256]{1,0:T(8,128)(2,1)} %query_v.1, ...), custom_call_target="tpu_custom_call" | custom-call | tf_op jit(solution)/shard_map/star/pallas_call | solution.py:550
  55.6 0.0 copy-start
  55.6 4.0 %copy.11 = bf16[768,2048]{1,0:T(8,128)(2,1)} copy(bf16[768,2048]{1,0:T(8,128)(2,1)} %get-tuple-element.4) | data formatting | bytes 6291456
  59.6 0.0 copy-done
  59.6 0.6 %copy.12 = bf16[64,256]{1,0:T(8,128)(2,1)} copy(bf16[64,256]{1,0:T(8,128)(2,1)S(1)} %copy-done) | data formatting | bytes 65536
Async XLA Ops:
  55.6 4.0 %copy-start = (bf16[64,256]{1,0:T(8,128)(2,1)S(1)}, bf16[64,256]{1,0:T(8,128)(2,1)}, u32[]{:S(2)}) copy-start(bf16[64,256]{1,0:T(8,128)(2,1)} %get-tuple-element.5) | copy-start | bytes 98308
